TPU v7x, 256 devices: a whole 4x4x8 slice. The times are simulated.
256 devices in a mesh: wide: 64 (over x, z, y_lo), kv: 4 (over y_hi, core).
Axes of the slice: x: 4, y: 4 (y_hi: 2, y_lo: 2; y = y_hi * 2 + y_lo), z: 8, core: 2. Of those that a mesh axis runs over, the one named last changes fastest.
Arguments:
- prompt_q: bfloat16 [4096, 8192], P('wide', 'kv'), may hold values from -2 to 2
- prompt_k: bfloat16 [4096, 512], P('wide', 'kv'), may hold values from -2 to 2
- prompt_v: bfloat16 [4096, 512], P('wide', 'kv'), may hold values from -6 to 6
- prompt_out: bfloat16 [4096, 8192], P('wide', 'kv'), may hold values from -6 to 6
- prompt_dout: bfloat16 [4096, 8192], P('wide', 'kv'), may hold values from -6 to 6
- resp_q: bfloat16 [4096, 8192], P('wide', 'kv'), may hold values from -2 to 2
- resp_k: bfloat16 [4096, 512], P('wide', 'kv'), may hold values from -2 to 2
- resp_v: bfloat16 [4096, 512], P('wide', 'kv'), may hold values from -6 to 6
- resp_out: bfloat16 [4096, 8192], P('wide', 'kv'), may hold values from -6 to 6
- resp_dout: bfloat16 [4096, 8192], P(('wide', 'kv')), may hold values from -6 to 6
- resp_len: int32 [64], P('wide'), may hold values from 1 to 64, 2560 in all
- loss_mask: int32 [4096], P('wide'), may hold values 0 or 1
Outputs:
- prompt_dq: float32 [4096, 8192], P('wide', 'kv')
- prompt_dk: float32 [4096, 512], P('wide', 'kv')
- prompt_dv: float32 [4096, 512], P('wide', 'kv')
- resp_dq: float32 [4096, 8192], P('wide', 'kv')
- resp_dk: float32 [4096, 512], P('wide', 'kv')
- resp_dv: float32 [4096, 512], P('wide', 'kv')
Inputs may be any that keep to these rules, and one draw needn't show every extreme that they name: Response m has resp_len[m] real tokens; slots from resp_len[m] on are padding; the longest response has exactly 64 tokens.
All inputs are finite; a program needn't handle non-finite values. No bound on the sum of `resp_len` or of `loss_mask` on one device may be relied on, other than what follows from the above.
Results may differ from a plain program's by a relative error of at most 0.0029.
Values may be sent and summed in bfloat16 or wider, within the bound.
A program may use at most 64 MiB of HBM per device.

v0:
```python
import math

import jax
import jax.numpy as jnp
from jax import lax
from jax.sharding import PartitionSpec as P


def blockwise(row_count, block_step, initial):
    block_size = 512
    block_count = row_count // block_size

    def loop_step(number, running):
        return block_step(running, number * block_size, block_size)

    return lax.fori_loop(0, block_count, loop_step, initial)


def key_scores(queries, key_rows, score_scale):
    return (
        jnp.einsum("nhd,kd->nhk", queries, key_rows, preferred_element_type=jnp.float32)
        * score_scale
    )


def visible(query_pos, key_pos):
    return key_pos[None, None, :] <= query_pos[:, None, None]


def exp_sums(queries, query_pos, key_rows, key_pos, score_scale):
    scores = key_scores(queries, key_rows, score_scale)
    return jnp.sum(jnp.where(visible(query_pos, key_pos), jnp.exp(scores), 0.0), axis=2)


def block_grads(
    queries, cotangents, row_dots, log_norm, query_pos, key_rows, value_rows, key_pos, score_scale
):
    scores = key_scores(queries, key_rows, score_scale)
    weights = jnp.where(visible(query_pos, key_pos), jnp.exp(scores - log_norm[:, :, None]), 0.0)
    weight_grad = jnp.einsum(
        "nhd,kd->nhk", cotangents, value_rows, preferred_element_type=jnp.float32
    )
    score_grad = (weights * (weight_grad - row_dots[:, :, None])).astype(jnp.bfloat16)
    query_grad = (
        jnp.einsum("nhk,kd->nhd", score_grad, key_rows, preferred_element_type=jnp.float32)
        * score_scale
    )
    key_grad = (
        jnp.einsum("nhk,nhd->kd", score_grad, queries, preferred_element_type=jnp.float32)
        * score_scale
    )
    value_grad = jnp.einsum(
        "nhk,nhd->kd", weights.astype(jnp.bfloat16), cotangents, preferred_element_type=jnp.float32
    )
    return (query_grad, jnp.concatenate([key_grad, value_grad], axis=1))


def sum_over(queries, query_pos, key_rows, first_key, score_scale, running):

    def sum_step(totals, begin, block_size):
        key_block = lax.dynamic_slice_in_dim(key_rows, begin, block_size, 0)
        key_pos = first_key + begin + jnp.arange(block_size, dtype=jnp.int32)
        return totals + exp_sums(queries, query_pos, key_block, key_pos, score_scale)

    return blockwise(key_rows.shape[0], sum_step, running)


def grads_over(
    queries,
    cotangents,
    row_dots,
    log_norm,
    query_pos,
    key_rows,
    value_rows,
    first_key,
    score_scale,
    running,
):

    def grad_step(totals, begin, block_size):
        query_total, key_total = totals
        key_block = lax.dynamic_slice_in_dim(key_rows, begin, block_size, 0)
        value_block = lax.dynamic_slice_in_dim(value_rows, begin, block_size, 0)
        key_pos = first_key + begin + jnp.arange(block_size, dtype=jnp.int32)
        query_part, key_part = block_grads(
            queries,
            cotangents,
            row_dots,
            log_norm,
            query_pos,
            key_block,
            value_block,
            key_pos,
            score_scale,
        )
        return (
            query_total + query_part,
            lax.dynamic_update_slice_in_dim(key_total, key_part, first_key + begin, 0),
        )

    return blockwise(key_rows.shape[0], grad_step, running)


def local(
    prompt_q,
    prompt_k,
    prompt_v,
    prompt_out,
    prompt_dout,
    resp_q,
    resp_k,
    resp_v,
    resp_out,
    resp_dout,
    resp_len,
    loss_mask,
):
    head_dim = prompt_k.shape[1]
    prompt_rows = prompt_q.shape[0]
    resp_rows = resp_q.shape[0]
    head_count = prompt_q.shape[1] // head_dim
    prompt_total = prompt_rows * lax.axis_size("wide")
    score_scale = 1.0 / math.sqrt(head_dim)
    arrived = lax.all_to_all(resp_dout, "kv", split_axis=1, concat_axis=0, tiled=True)
    positions = jnp.arange(resp_rows, dtype=jnp.int32)
    usable = (positions < resp_len[0]) & (loss_mask == 1)
    resp_cot = jnp.where(usable[:, None], arrived, jnp.zeros_like(arrived))
    query_count = prompt_rows + resp_rows
    queries = jnp.concatenate([prompt_q, resp_q], axis=0).reshape(query_count, head_count, head_dim)
    cotangents = jnp.concatenate([prompt_dout, resp_cot], axis=0).reshape(
        query_count, head_count, head_dim
    )
    forward_out = jnp.concatenate([prompt_out, resp_out], axis=0).reshape(
        query_count, head_count, head_dim
    )
    own_pos = prompt_total + positions
    query_pos = jnp.concatenate(
        [lax.axis_index("wide") * prompt_rows + jnp.arange(prompt_rows, dtype=jnp.int32), own_pos]
    )
    row_dots = jnp.sum(cotangents.astype(jnp.float32) * forward_out.astype(jnp.float32), axis=2)
    own_sums = exp_sums(queries, query_pos, resp_k, own_pos, score_scale)
    zero_grad = jnp.zeros((query_count, head_count, head_dim), jnp.float32)
    all_keys, all_values = (
        lax.all_gather(prompt_k, "wide", axis=0, tiled=True),
        lax.all_gather(prompt_v, "wide", axis=0, tiled=True),
    )
    totals = sum_over(queries, query_pos, all_keys, 0, score_scale, own_sums)
    log_norm = jnp.log(totals)
    key_buffer = jnp.zeros((prompt_total, 2 * head_dim), jnp.float32)
    query_total, key_total = grads_over(
        queries,
        cotangents,
        row_dots,
        log_norm,
        query_pos,
        all_keys,
        all_values,
        0,
        score_scale,
        (zero_grad, key_buffer),
    )
    prompt_sums = lax.psum_scatter(key_total, "wide", scatter_dimension=0, tiled=True)
    own_query, own_keys = block_grads(
        queries, cotangents, row_dots, log_norm, query_pos, resp_k, resp_v, own_pos, score_scale
    )
    query_grad = query_total + own_query
    prompt_dq = query_grad[:prompt_rows].reshape(prompt_rows, head_count * head_dim)
    resp_dq = query_grad[prompt_rows:].reshape(resp_rows, head_count * head_dim)
    return (
        prompt_dq,
        prompt_sums[:, :head_dim],
        prompt_sums[:, head_dim:],
        resp_dq,
        own_keys[:, :head_dim],
        own_keys[:, head_dim:],
    )


def solution(mesh):
    return jax.shard_map(
        local,
        mesh=mesh,
        in_specs=(
            P("wide", "kv"),
            P("wide", "kv"),
            P("wide", "kv"),
            P("wide", "kv"),
            P("wide", "kv"),
            P("wide", "kv"),
            P("wide", "kv"),
            P("wide", "kv"),
            P("wide", "kv"),
            P(("wide", "kv"), None),
            P("wide"),
            P("wide"),
        ),
        out_specs=(
            P("wide", "kv"),
            P("wide", "kv"),
            P("wide", "kv"),
            P("wide", "kv"),
            P("wide", "kv"),
            P("wide", "kv"),
        ),
        check_vma=False,
    )
```

profile of v0, /device:TPU:16, one launch (start us, length us, event | category | flops | bytes accessed | tf_op | source)
XLA Modules:
  0.0 1007.0 jit_solution(8034629034642249209)
XLA Ops:
  9.6 5.4 all-to-all-start
  27.5 282.0 %all-gather.3.cloned.1.call-done = bf16[4096,128]{1,0:T(8,128)(2,1)} async-done(((bf16[64,128]{1,0:T(8,128)(2,1)}), bf16[4096,128]{1,0:T(8,128)(2,1)}) %all-gather.3.cloned.1.call-update) | async-done | bytes 1048592 | tf_op jit(solution)/shard_map/all_gather | solution.py:145
  309.5 18.4 %while.29 = (s32[]{:T(128)}, f32[128,16]{0,1:T(8,128)S(1)}, s32[128]{0:T(128)S(1)}, bf16[4096,128]{1,0:T(8,128)(2,1)}, bf16[128,16,128]{2,0,1:T(8,128)(2,1)}, /*index=5*/s32[]{:T(128)}, s32[]{:T(128)}, s32[]{:T(128)}, s32[]{:T(128)}) while((s32[]{:T(128)}, f32[128,16]{0,1:T(8,128)S(1)}, s32[128]{0:T(128)S(1)}, bf16[4096,128]{1,0:T(8,128)(2,1)}, ...), condition=%wide.region_3.4_spmd, body=%wide.region_1.3_spmd.sunk | while | flops 271647232 | bytes 823955 | solution.py:16
  309.7 2.1 fusion.74
  312.0 2.1 fusion.74
  314.3 2.1 fusion.74
  316.6 2.1 fusion.74
  318.9 2.1 fusion.74
  321.2 2.1 fusion.74
  323.5 2.1 fusion.74
  325.8 2.1 fusion.74
  327.9 277.5 %all-gather.5.cloned.1.call-done = bf16[4096,128]{1,0:T(8,128)(2,1)} async-done(((bf16[64,128]{1,0:T(8,128)(2,1)}), bf16[4096,128]{1,0:T(8,128)(2,1)}) %all-gather.5.cloned.1.call-update) | async-done | bytes 1048592 | tf_op jit(solution)/shard_map/all_gather | solution.py:146
  605.4 2.2 broadcast_in_dim.107.clone
  607.6 72.2 %while.30 = (s32[]{:T(128)}, f32[128,16,128]{2,0,1:T(8,128)S(1)}, f32[4096,256]{1,0:T(8,128)}, s32[128]{0:T(128)S(1)}, bf16[4096,128]{1,0:T(8,128)(2,1)}, /*inde...) while((s32[]{:T(128)}, f32[128,16,128]{2,0,1:T(8,128)S(1)}, ...), condition=%wide.region_6.7_spmd.clone, body=%wide.region_5.6_spmd.clone.sunk | while | flops 1353712128 | bytes 27357912 | solution.py:16
  610.3 2.3 fusion.86
  619.4 2.3 fusion.86
  628.4 2.3 fusion.86
  631.5 2.1 fusion.87
  637.4 2.3 fusion.86
  646.5 2.3 fusion.86
  655.5 2.3 fusion.86
  664.5 2.3 fusion.86
  673.5 2.3 fusion.86
  685.1 314.0 %reduce-scatter.2.cloned.1.call-done = f32[64,256]{1,0:T(8,128)} async-done(((f32[4096,256]{1,0:T(8,128)}), f32[64,256]{1,0:T(8,128)}) %reduce-scatter.2.cloned.1.call-update) | async-done | bytes 65552 | tf_op jit(solution)/shard_map/reduce_scatter | solution.py:163
  (136 shorter events, 73.2 us)
Async XLA Ops:
  7.2 15.7 %copy-start = (bf16[64,128]{1,0:T(8,128)(2,1)S(1)}, bf16[64,128]{1,0:T(8,128)(2,1)}, u32[]{:S(2)}) copy-start(bf16[64,128]{1,0:T(8,128)(2,1)} %param.22) | copy-start | bytes 49156
  7.2 16.8 %copy-start.3 = (s32[64]{0:T(128)S(1)}, s32[64]{0:T(128)}, u32[]{:S(2)}) copy-start(s32[64]{0:T(128)} %param.27) | copy-start | bytes 772
  7.2 302.3 %all-gather.3.cloned.1.call-start = ((), (), s32[]{:S(2)}) async-start(), calls=%async_computation.2 | async-start | bytes 1064960 | tf_op jit(solution)/shard_map/all_gather | solution.py:145
  9.6 14.4 %all-to-all-start = ((bf16[16,4,2048]{2,0,1:T(8,128)(2,1)}), bf16[16,4,2048]{2,0,1:T(8,128)(2,1)S(1)}, u32[]{:S(2)}, u32[]{:S(2)}) async-start(bf16[16,4,2048]{2,0,1:T(8,128)(2,1)} %bitcast.87), calls=%async_computation | async-start | bytes 524288 | tf_op jit(solution)/shard_map/all_to_all | solution.py:125
  15.0 590.4 %all-gather.5.cloned.1.call-start = ((), (), s32[]{:S(2)}) async-start(), calls=%async_computation.3 | async-start | bytes 1064960 | tf_op jit(solution)/shard_map/all_gather | solution.py:146
  15.8 983.3 %reduce-scatter.2.cloned.1.call-start = ((), (), s32[]{:S(2)}) async-start(), calls=%async_computation.4 | async-start | bytes 4259840 | tf_op jit(solution)/shard_map/reduce_scatter | solution.py:163
  679.8 1.0 copy-start.1
  679.8 1.0 copy-start.2
Sparse Core Ops, SparseCore 0:
  9.8 299.6 all-gather.2
  311.3 294.0 all-gather.4
  680.0 318.9 reduce-scatter.1
where the time goes:
time: 1010 us
  waiting for transfers between devices  875 us (87%)
  matrix products  82.4 us (8%)
  local copies, waits for them, and re-layouts  23.6 us (2%)
  between operations  14.5 us (1%)
    reduce_scatter x1, waiting for transfers between devices, local(): lax.psum_scatter(key_total, 'wide', scatter_dimension=0, tiled=True)  314 us
    all_gather x1, waiting for transfers between devices, local(): lax.all_gather(prompt_k, 'wide', axis=0, tiled=True)  282 us
    all_gather x1, waiting for transfers between devices, local(): lax.all_gather(prompt_v, 'wide', axis=0, tiled=True)  278 us
    dot_general x17, matrix products, key_scores(): jnp.einsum('nhd,kd->nhk', queries, key_rows, preferred_element_type=jnp.f...  30.7 us
  transfers between devices with their start and end apart: 4, of which 3 were waited for; matrix products, arithmetic and copies ran while one was open for 3% of the time, Pallas kernels for 0%

commit v1 on v0

v1 whole, which is shorter than its diff:
```python
import functools
import math

import jax
import jax.numpy as jnp
from jax import lax
from jax.experimental import pallas as pl
from jax.experimental.pallas import tpu as pltpu
from jax.sharding import PartitionSpec as P

MESH = pl.DeviceIdType.MESH
BF = jnp.bfloat16
F32 = jnp.float32
NX, NZ, NY = 4, 8, 2
R = 64
D = 128
H = 16
ROWS = H * R
SCALE = 1.0 / math.sqrt(D)
EXP2_SCALE = math.log2(math.e) / math.sqrt(D)
HALF = NX * NZ * R
ABLK = NX * R
BBLK = NZ * R
NN = (((1,), (0,)), ((), ()))
NT = (((1,), (1,)), ((), ()))
TN = (((0,), (0,)), ((), ()))
COPIES = 48
DEFER = 4


def dot(a, b, dims):
    return lax.dot_general(a, b, dims, preferred_element_type=F32)


def by_head(ref):
    return jnp.concatenate([ref[:, h * D : (h + 1) * D] for h in range(H)], axis=0)


def lane_dots(a, b):
    prod = a.astype(F32) * b.astype(F32)
    high = prod.astype(BF)
    low = (prod - high.astype(F32)).astype(BF)
    ones = jnp.ones((8, D), BF)
    return dot(ones, high, NT) + dot(ones, low, NT)


def gray(t):
    return t + (t // 2) * (1 - 2 * lax.rem(t, 2))


def kernel(
    pq, pk, pv, po, pdo, rq, rk, rv, ro, rdo, rlen, lmask,
    pdq, pdk, pdv, rdq, rdk, rdv,
    kvb, qs, dos, arrived, e, eo, dss, zs, dvec, dqt, part, acc_a, acc_b,
    s_r, s_l, r_r, r_l, sb_r, sb_l, rb_r, rb_l, xa_r, zb_s, zb_r, tot, yr,
    ssem, rsem,
):
    w, kv = lax.axis_index("wide"), lax.axis_index("kv")
    x, z, y = w // (NZ * NY), lax.rem(w // NY, NZ), lax.rem(w, NY)

    def dev(xx, zz, yy, vv):
        return ((xx * NZ + zz) * NY + yy, vv)

    def xp(i):
        return dev(lax.rem(x + i, NX), z, y, kv)

    def zp(i):
        return dev(x, lax.rem(z + i, NZ), y, kv)

    yp = dev(x, z, 1 - y, kv)

    def vp(i):
        return dev(x, z, y, lax.rem(kv + i, 4))

    barrier = pltpu.get_barrier_semaphore()
    peers = [yp] + [xp(i) for i in range(1, NX)] + [zp(i) for i in range(1, NZ)] + [vp(i) for i in range(1, 4)]
    for peer in peers:
        pl.semaphore_signal(barrier, inc=1, device_id=peer, device_id_type=MESH)

    sem_no = {}

    def copy(key, src, dst, to):
        i = sem_no.setdefault(key, len(sem_no))
        return pltpu.make_async_remote_copy(
            src_ref=src, dst_ref=dst, send_sem=ssem.at[i], recv_sem=rsem.at[i],
            device_id=to, device_id_type=MESH,
        )

    def off_a(zz):
        return pl.multiple_of(zz * ABLK, ABLK)

    def off_b(xx):
        return pl.multiple_of(HALF + xx * BBLK, BBLK)

    def rows(off, n):
        return kvb.at[pl.ds(pl.multiple_of(off, R), n)]

    own = (1 - y) * (z * ABLK + x * R) + y * (HALF + x * BBLK + z * R)

    def g_y():
        return copy("gy", rows(own, R), rows(own, R), yp)

    def g_ax(i):
        b = rows(z * ABLK + x * R, R)
        return copy(("gax", i), b, b, xp(i))

    def g_bz(i):
        b = rows(HALF + x * BBLK + z * R, R)
        return copy(("gbz", i), b, b, zp(i))

    def g_zr(right, s):
        zz = lax.rem(z + (NZ - s if right else s), NZ)
        if s < 3:
            b = rows(zz * ABLK, ABLK)
        elif right:
            b = rows(zz * ABLK, ABLK // 2)
        else:
            b = rows(zz * ABLK + ABLK // 2, ABLK // 2)
        return copy(("gzr", right, s), b, b, zp(1 if right else NZ - 1))

    def g_xr(right, s):
        xx = lax.rem(x + (NX - s if right else s), NX)
        if s < 1:
            b = rows(HALF + xx * BBLK, BBLK)
        elif right:
            b = rows(HALF + xx * BBLK, BBLK // 2)
        else:
            b = rows(HALF + xx * BBLK + BBLK // 2, BBLK // 2)
        return copy(("gxr", right, s), b, b, xp(1 if right else NX - 1))

    def g_v(i):
        col = pl.multiple_of(lax.rem(kv + i, 4) * (H * D), H * D)
        return copy(
            ("gv", i),
            rdo.at[:, pl.ds(col, H * D)],
            arrived.at[pl.ds(pl.multiple_of(kv * 16, 16), 16)],
            vp(i),
        )

    def t_zr(right, t):
        if right:
            return copy(("tzr", t), s_r.at[t], r_r.at[t], zp(1))
        return copy(("tzl", t), s_l.at[t], r_l.at[t], zp(NZ - 1))

    def t_xr(right, t):
        if right:
            return copy(("txr", t), sb_r.at[t], rb_r.at[t], xp(1))
        return copy(("txl", t), sb_l, rb_l, xp(NX - 1))

    def t_ax(i):
        src = acc_a.at[pl.ds(pl.multiple_of(lax.rem(x + i, NX) * R, R), R)]
        return copy(("tax", i), src, xa_r.at[i], xp(i))

    def t_bz(i):
        return copy(("tbz", i), zb_s.at[pl.ds(pl.multiple_of(lax.rem(z + i, NZ) * R, R), R)], zb_r.at[i], zp(i))

    def t_y():
        return copy("ty", tot.at[1 - y], yr, yp)

    kvb[pl.ds(pl.multiple_of(own, R), R), 0:D] = pk[...]
    kvb[pl.ds(pl.multiple_of(own, R), R), D : 2 * D] = pv[...]
    qs[0:ROWS] = by_head(pq)
    qs[ROWS : 2 * ROWS] = by_head(rq)
    prompt_cot = by_head(pdo)
    dos[0:ROWS] = prompt_cot
    dvec[:, 0:ROWS] = lane_dots(prompt_cot, by_head(po))
    dqt[...] = jnp.zeros_like(dqt)
    row_minus_col = lax.broadcasted_iota(jnp.int32, (R, ROWS), 0) - lax.rem(
        lax.broadcasted_iota(jnp.int32, (R, ROWS), 1), R
    )
    own_e = jnp.where(
        row_minus_col <= 0, jnp.exp2(dot(rk[...], qs[ROWS : 2 * ROWS], NT) * EXP2_SCALE), 0.0
    )
    eo[...] = own_e
    zs[:, 0:ROWS] = jnp.zeros((8, ROWS), F32)
    zs[:, ROWS : 2 * ROWS] = jnp.sum(own_e.reshape(R // 8, 8, ROWS), axis=0)
    pl.semaphore_wait(barrier, len(peers))

    g_y().start()
    for i in range(1, 4):
        g_v(i).start()
    arrived[pl.ds(pl.multiple_of(kv * 16, 16), 16), :] = rdo[:, pl.ds(pl.multiple_of(kv * (H * D), H * D), H * D)]
    g_y().wait_recv()
    for i in range(1, NX):
        g_ax(i).start()
    for i in (4, 3, 5, 2, 6, 1, 7):
        g_bz(i).start()
    for i in range(1, NX):
        g_ax(i).wait_recv()
    g_zr(True, 0).start()
    g_zr(False, 0).start()

    def first(j, carry):
        t, is_b = j // 2, 1 - lax.rem(j, 2)

        @pl.when(j == 0)
        def _():
            for i in range(1, NZ):
                g_bz(i).wait_recv()
            g_xr(True, 0).start()
            g_xr(False, 0).start()

        for s in range(4):

            @pl.when(j == 2 * s + 1)
            def _():
                g_zr(True, s).wait_recv()
                g_zr(False, s).wait_recv()
                if s < 3:
                    g_zr(True, s + 1).start()
                    g_zr(False, s + 1).start()

        @pl.when(j == 2)
        def _():
            g_xr(True, 0).wait_recv()
            g_xr(False, 0).wait_recv()
            g_xr(True, 1).start()
            g_xr(False, 1).start()

        @pl.when(j == 6)
        def _():
            g_xr(True, 1).wait_recv()
            g_xr(False, 1).wait_recv()

        za, zb = lax.rem(z + NZ - t - 1, NZ), lax.rem(z + lax.rem(t + 1, 4), NZ)
        xb = lax.rem(x + gray(t), NX)
        off1 = is_b * (HALF + xb * BBLK) + (1 - is_b) * (za * ABLK)
        off2 = is_b * (HALF + xb * BBLK + BBLK // 2) + (1 - is_b) * (zb * ABLK)
        stride = is_b * (NY * R) + (1 - is_b) * (NZ * NY * R)
        base1 = is_b * (xb * (NZ * NY * R) + R) + (1 - is_b) * (za * (NY * R))
        base2 = is_b * (xb * (NZ * NY * R) + (NZ // 2) * NY * R + R) + (1 - is_b) * (zb * (NY * R))
        off1, off2 = pl.multiple_of(off1, 256), pl.multiple_of(off2, 256)
        keys = jnp.concatenate([kvb[pl.ds(off1, 256), 0:D], kvb[pl.ds(off2, 256), 0:D]], axis=0)
        ex = jnp.exp2(dot(keys, qs[...], NT) * EXP2_SCALE)
        seen = []
        for g in range(8):
            limit = w * R - (base1 if g < 4 else base2) - (g % 4) * stride
            seen.append(jnp.where(row_minus_col <= limit, ex[g * R : (g + 1) * R, 0:ROWS], 0.0))
        seen = jnp.concatenate(seen, axis=0)
        rest = ex[:, ROWS : 2 * ROWS]
        for k, off in ((0, off1), (1, off2)):
            e[pl.ds(off, 256), 0:ROWS] = seen[k * 256 : (k + 1) * 256]
            e[pl.ds(off, 256), ROWS : 2 * ROWS] = rest[k * 256 : (k + 1) * 256]
        zs[:, 0:ROWS] += jnp.sum(seen.reshape(64, 8, ROWS), axis=0)
        zs[:, ROWS : 2 * ROWS] += jnp.sum(rest.reshape(64, 8, ROWS), axis=0)
        return carry

    lax.fori_loop(0, 8, first, 0)

    for i in range(1, 4):
        g_v(i).wait_recv()
    tokens = lax.broadcasted_iota(jnp.int32, (R, R), 1)
    usable = (lmask[...] == 1) & (lax.broadcasted_iota(jnp.int32, (1, R), 1) < rlen[0])
    diagonal = lax.broadcasted_iota(jnp.int32, (R, R), 0) == tokens
    keep = jnp.sum(jnp.where(diagonal & usable, 1.0, 0.0), axis=1, keepdims=True)
    keep = jnp.broadcast_to(keep, (R, D)) > 0.5
    keep = jnp.concatenate([keep] * H, axis=0)
    cot = jnp.where(keep, by_head(arrived).astype(F32), 0.0).astype(BF)
    dos[ROWS : 2 * ROWS] = cot
    dvec[:, ROWS : 2 * ROWS] = lane_dots(cot, by_head(ro))
    zs[...] = jnp.broadcast_to(1.0 / jnp.sum(zs[...], axis=0, keepdims=True), zs.shape)

    def second(j, carry):
        t, is_a = j // 2, 1 - lax.rem(j, 2)
        xb = lax.rem(x + gray(3 - t), NX)
        off1 = is_a * (lax.rem(z + 4 - t, NZ) * ABLK) + (1 - is_a) * (HALF + xb * BBLK)
        off2 = is_a * (lax.rem(z + 5 + t, NZ) * ABLK) + (1 - is_a) * (HALF + xb * BBLK + BBLK // 2)
        off1, off2 = pl.multiple_of(off1, 256), pl.multiple_of(off2, 256)
        pair = jnp.concatenate([kvb[pl.ds(off1, 256), :], kvb[pl.ds(off2, 256), :]], axis=0)
        keys, values = pair[:, 0:D], pair[:, D : 2 * D]
        ex = jnp.concatenate([e[pl.ds(off1, 256), :], e[pl.ds(off2, 256), :]], axis=0)
        weights = ex * zs[0:1, :]
        part[:, D : 2 * D] = dot(weights.astype(BF), dos[...], NN)
        weight_grad = dot(values, dos[...], NT)
        score_grad = (weights * (weight_grad - dvec[0:1, :])).astype(BF)
        part[:, 0:D] = dot(score_grad, qs[...], NN)

        @pl.when(j < 8 - DEFER)
        def _():
            dqt[...] += dot(keys, score_grad, TN)

        @pl.when(j >= 8 - DEFER)
        def _():
            dss[pl.ds(pl.multiple_of((j - (8 - DEFER)) * 512, 512), 512), :] = score_grad

        for s in range(4):

            @pl.when(j == 2 * s)
            def _():
                right, left = part[0:256, :], part[256:512, :]
                if s > 0:
                    t_zr(True, s - 1).wait_recv()
                    t_zr(False, s - 1).wait_recv()
                    right = right + r_r[s - 1].astype(F32)
                    left = left + r_l[s - 1].astype(F32)
                s_r[s] = right.astype(BF)
                t_zr(True, s).start()
                if s < 3:
                    s_l[s] = left.astype(BF)
                    t_zr(False, s).start()
                else:
                    acc_a[...] = left

        @pl.when(j == 1)
        def _():
            sb_r[0] = part[...].astype(BF)
            t_xr(True, 0).start()

        @pl.when(j == 3)
        def _():
            sb_l[...] = part[...].astype(BF)
            t_xr(False, 0).start()

        @pl.when(j == 5)
        def _():
            t_xr(True, 0).wait_recv()
            sb_r[1] = (part[...] + rb_r[0].astype(F32)).astype(BF)
            t_xr(True, 1).start()

        @pl.when(j == 7)
        def _():
            t_xr(True, 1).wait_recv()
            t_xr(False, 0).wait_recv()
            acc = part[...] + rb_r[1].astype(F32) + rb_l[...].astype(F32)
            acc_b[...] = acc
            zb_s[...] = acc.astype(BF)
            for i in (4, 3, 5, 2, 6, 1, 7):
                t_bz(i).start()

        return carry

    lax.fori_loop(0, 8, second, 0)

    def late(i, carry):
        j = i + (8 - DEFER)
        t, is_a = j // 2, 1 - lax.rem(j, 2)
        xb = lax.rem(x + gray(3 - t), NX)
        off1 = is_a * (lax.rem(z + 4 - t, NZ) * ABLK) + (1 - is_a) * (HALF + xb * BBLK)
        off2 = is_a * (lax.rem(z + 5 + t, NZ) * ABLK) + (1 - is_a) * (HALF + xb * BBLK + BBLK // 2)
        off1, off2 = pl.multiple_of(off1, 256), pl.multiple_of(off2, 256)
        keys = jnp.concatenate([kvb[pl.ds(off1, 256), 0:D], kvb[pl.ds(off2, 256), 0:D]], axis=0)
        dqt[...] += dot(keys, dss[pl.ds(pl.multiple_of(i * 512, 512), 512), :], TN)

        @pl.when(i == DEFER // 2 - 1)
        def _():
            t_zr(True, 3).wait_recv()
            acc_a[...] += r_r[3].astype(F32)
            for k in range(1, NX):
                t_ax(k).start()

        return carry

    lax.fori_loop(0, DEFER, late, 0)

    own_w = eo[...] * zs[0:1, ROWS : 2 * ROWS]
    rdv[...] = dot(own_w.astype(BF), dos[ROWS : 2 * ROWS], NN)
    own_g = dot(rv[...], dos[ROWS : 2 * ROWS], NT) - dvec[0:1, ROWS : 2 * ROWS]
    own_g = (own_w * own_g).astype(BF)
    rdk[...] = dot(own_g, qs[ROWS : 2 * ROWS], NN) * SCALE
    dqt[:, ROWS : 2 * ROWS] += dot(rk[...], own_g, TN)

    for i in range(1, NX):
        t_ax(i).wait_recv()
    total = acc_a[pl.ds(pl.multiple_of(x * R, R), R), :]
    for i in range(1, NX):
        total = total + xa_r[i]
    tot[0] = total
    for i in range(1, NZ):
        t_bz(i).wait_recv()
    total = acc_b[pl.ds(pl.multiple_of(z * R, R), R), :]
    for i in range(1, NZ):
        total = total + zb_r[i].astype(F32)
    tot[1] = total
    t_y().start()
    for h in range(0, H, 2):
        for out, first_col in ((pdq, 0), (rdq, ROWS)):
            block = dqt[:, first_col + h * R : first_col + (h + 2) * R].T * SCALE
            out[:, h * D : (h + 1) * D] = block[0:R]
            out[:, (h + 1) * D : (h + 2) * D] = block[R : 2 * R]
    t_y().wait_recv()
    final = tot[y] + yr[...]
    pdk[...] = final[:, 0:D] * SCALE
    pdv[...] = final[:, D : 2 * D]

    g_y().wait_send()
    t_y().wait_send()
    for i in range(1, NX):
        g_ax(i).wait_send()
        t_ax(i).wait_send()
    for i in range(1, NZ):
        g_bz(i).wait_send()
        t_bz(i).wait_send()
    for i in range(1, 4):
        g_v(i).wait_send()
    for s in range(4):
        g_zr(True, s).wait_send()
        g_zr(False, s).wait_send()
        t_zr(True, s).wait_send()
        if s < 3:
            t_zr(False, s).wait_send()
    for s in range(2):
        g_xr(True, s).wait_send()
        g_xr(False, s).wait_send()
        t_xr(True, s).wait_send()
    t_xr(False, 0).wait_send()


def local(
    prompt_q, prompt_k, prompt_v, prompt_out, prompt_dout,
    resp_q, resp_k, resp_v, resp_out, resp_dout, resp_len, loss_mask,
):
    vmem = pl.BlockSpec(memory_space=pltpu.VMEM)
    smem = pl.BlockSpec(memory_space=pltpu.SMEM)
    wide_out = jax.ShapeDtypeStruct((R, H * D), F32)
    head_out = jax.ShapeDtypeStruct((R, D), F32)
    V = pltpu.VMEM
    return pl.pallas_call(
        kernel,
        out_shape=[wide_out, head_out, head_out, wide_out, head_out, head_out],
        in_specs=[vmem] * 10 + [smem, vmem],
        out_specs=[vmem] * 6,
        scratch_shapes=[
            V((2 * HALF, 2 * D), BF),
            V((2 * ROWS, D), BF),
            V((2 * ROWS, D), BF),
            V((R, H * D), BF),
            V((2 * HALF, 2 * ROWS), F32),
            V((R, ROWS), F32),
            V((DEFER * 512, 2 * ROWS), BF),
            V((8, 2 * ROWS), F32),
            V((8, 2 * ROWS), F32),
            V((D, 2 * ROWS), F32),
            V((512, 2 * D), F32),
            V((ABLK, 2 * D), F32),
            V((BBLK, 2 * D), F32),
            V((4, ABLK, 2 * D), BF),
            V((3, ABLK, 2 * D), BF),
            V((4, ABLK, 2 * D), BF),
            V((3, ABLK, 2 * D), BF),
            V((2, BBLK, 2 * D), BF),
            V((BBLK, 2 * D), BF),
            V((2, BBLK, 2 * D), BF),
            V((BBLK, 2 * D), BF),
            V((NX, R, 2 * D), F32),
            V((BBLK, 2 * D), BF),
            V((NZ, R, 2 * D), BF),
            V((2, R, 2 * D), F32),
            V((R, 2 * D), F32),
            pltpu.SemaphoreType.DMA((COPIES,)),
            pltpu.SemaphoreType.DMA((COPIES,)),
        ],
        compiler_params=pltpu.CompilerParams(
            collective_id=0, has_side_effects=True, vmem_limit_bytes=62 * 2**20
        ),
    )(
        prompt_q, prompt_k, prompt_v, prompt_out, prompt_dout,
        resp_q, resp_k, resp_v, resp_out, resp_dout, resp_len, loss_mask.reshape(1, R),
    )


def solution(mesh):
    grid = P("wide", "kv")
    return jax.shard_map(
        local,
        mesh=mesh,
        in_specs=(grid,) * 9 + (P(("wide", "kv"), None), P("wide"), P("wide")),
        out_specs=(grid,) * 6,
        check_vma=False,
    )
```

time: 1010 us -> 80.2 us (0.08)
  waiting for transfers between devices: 875 us -> 0 us
  matrix products: 82.4 us -> 0 us
  Pallas kernels: 0 us -> 72.8 us
  local copies, waits for them, and re-layouts: 23.6 us -> 5.5 us
  between operations: 14.5 us -> 1.31 us
    all_gather x2 -> x0, waiting for transfers between devices: 559 us -> none  [the longest x1 282 us: local(): lax.all_gather(prompt_k, 'wide', axis=0, tiled=True)]
    reduce_scatter x1 -> x0, waiting for transfers between devices: 314 us -> none  [local(): lax.psum_scatter(key_total, 'wide', scatter_dimension=0, tiled=True)]
    dot_general x53 -> x0, matrix products: 82.4 us -> none  [the longest x17 30.7 us: key_scores(): jnp.einsum('nhd,kd->nhk', queries, key_rows, preferred_element_type=jnp.f...]
    pallas_call x0 -> x1, Pallas kernels: none -> 72.8 us  [local(): pl.pallas_call(kernel, out_shape=[wide_out, head_out, head_out, wide_out,...]
  transfers between devices with their start and end apart: 4 -> 0, of which waited for: 3 -> 0; matrix products, arithmetic and copies ran while one was open for 3% -> 0% of each run, Pallas kernels for 0% -> 0%
where the time goes in v1:
time: 80.2 us; the launch traced here: 79.7 us
  Pallas kernels  72.8 us (91%)
  local copies, waits for them, and re-layouts  5.5 us (7%)
  between operations  1.31 us (2%)
    pallas_call x1, Pallas kernels, local(): pl.pallas_call(kernel, out_shape=[wide_out, head_out, head_out, wide_out,...  72.8 us
    unnamed x16, local copies, waits for them, and re-layouts  5.5 us

profile of v1, /device:TPU:16, one launch (start us, length us, event | category | flops | bytes accessed | tf_op | source)
XLA Modules:
  0.0 79.7 jit_solution(4295728374640062151)
XLA Ops:
  1.3 72.8 %shard_map.163 = (f32[64,2048]{1,0:T(8,128)}, f32[64,128]{1,0:T(8,128)}, f32[64,128]{1,0:T(8,128)}, f32[64,2048]{1,0:T(8,128)}, f32[64,128]{1,0:T(8,128)}, /*index=5*/f32[64,128]{1,0:T(8,128)}) custom-call(bf16[64,2048]{1,0:T(8,128)(2,1)} %pq.1, bf16[64,128]{1,0:T(8,128)(2,1)} %pk.1, bf16[64,128]{1,0:T(8,128)(2,1)} %pv.1, bf16[64,2048]{1,0:T(8,128)(2,1)} %po.1, ...), custom_call_target="tpu_custom_call" | custom-call | tf_op jit(solution)/shard_map/pallas_call | solution.py:417
  74.1 0.0 copy-start.4
  74.1 0.0 copy-start
  74.1 1.9 %copy.25 = f32[64,2048]{1,0:T(8,128)} copy(f32[64,2048]{1,0:T(8,128)} %get-tuple-element.12) | data formatting | bytes 1048576
  76.1 0.0 copy-done.4
  76.1 0.0 copy-start.3
  76.1 0.6 copy.26
  76.7 0.2 copy-done.3
  76.9 0.6 copy.27
  77.5 0.0 copy-done
  77.5 0.0 copy-start.2
  77.5 0.8 copy.28
  78.3 0.0 copy-done.2
  78.3 0.0 copy-start.1
  78.3 0.6 copy.29
  78.9 0.2 copy-done.1
  79.0 0.6 copy.30
Async XLA Ops:
  74.1 2.0 %copy-start.4 = (f32[64,128]{1,0:T(8,128)S(1)}, f32[64,128]{1,0:T(8,128)}, u32[]{:S(2)}) copy-start(f32[64,128]{1,0:T(8,128)} %get-tuple-element.13) | copy-start | bytes 98308
  74.1 3.3 %copy-start = (f32[64,2048]{1,0:T(8,128)S(1)}, f32[64,2048]{1,0:T(8,128)}, u32[]{:S(2)}) copy-start(f32[64,2048]{1,0:T(8,128)} %get-tuple-element.15) | copy-start | bytes 1572868
  76.1 0.8 copy-start.3
  77.5 0.8 %copy-start.2 = (f32[64,128]{1,0:T(8,128)S(1)}, f32[64,128]{1,0:T(8,128)}, u32[]{:S(2)}) copy-start(f32[64,128]{1,0:T(8,128)} %get-tuple-element.16) | copy-start | bytes 98308
  78.3 0.8 copy-start.1

commit v2 on v1

v2 whole, which is shorter than its diff:
```python
import functools
import math

import jax
import jax.numpy as jnp
from jax import lax
from jax.experimental import pallas as pl
from jax.experimental.pallas import tpu as pltpu
from jax.sharding import PartitionSpec as P

MESH = pl.DeviceIdType.MESH
BF = jnp.bfloat16
F32 = jnp.float32
NX, NZ, NY = 4, 8, 2
NU = NX * NY
R = 64
S = R // 2
D = 128
H = 16
ROWS = H * R
SCALE = 1.0 / math.sqrt(D)
EXP2_SCALE = math.log2(math.e) / math.sqrt(D)
HALF = NU * NZ * S
BLK = NU * S
SUBS = 4
PIECE = BLK // SUBS
SUMS = 2
SUM_PIECE = BLK // SUMS
NN = (((1,), (0,)), ((), ()))
NT = (((1,), (1,)), ((), ()))
TN = (((0,), (0,)), ((), ()))
COPIES = 87
EARLY = 2


def dot(a, b, dims):
    return lax.dot_general(a, b, dims, preferred_element_type=F32)


def by_head(ref):
    return jnp.concatenate([ref[:, h * D : (h + 1) * D] for h in range(H)], axis=0)


def lane_dots(a, b):
    prod = a.astype(F32) * b.astype(F32)
    high = prod.astype(BF)
    low = (prod - high.astype(F32)).astype(BF)
    ones = jnp.ones((8, D), BF)
    return dot(ones, high, NT) + dot(ones, low, NT)


def kernel(
    pq_hbm, pk_hbm, pv_hbm, po_hbm, pdo_hbm, rq_hbm, rk_hbm, rv_hbm, ro_hbm, rdo_hbm, rlen, lmask,
    dq_hbm, kvg_hbm,
    pq, pk, pv, po, pdo, rq, rk, rv, ro, rdo, dq, kvg,
    kvb, qs, dos, arrived, e, eo, dss, zs, dvec, dqt, part, acc_p, acc_q,
    s_r, s_l, r_r, r_l, sq, rq_in, sp_out, rp_in, sz_out, rz_in,
    ssem, rsem, lsem, osem,
):
    w, kv = lax.axis_index("wide"), lax.axis_index("kv")
    x, z, y = w // (NZ * NY), lax.rem(w // NY, NZ), lax.rem(w, NY)
    u = x * NY + y

    def dev(uu, zz, vv):
        return (((uu // NY) * NZ + zz) * NY + lax.rem(uu, NY), vv)

    def up(i):
        return dev(lax.rem(u + i, NU), z, kv)

    def zp(i):
        return dev(u, lax.rem(z + i, NZ), kv)

    def vp(i):
        return dev(u, z, lax.rem(kv + i, 4))

    barrier = pltpu.get_barrier_semaphore()
    peers = [zp(i) for i in range(1, NZ)] + [up(i) for i in range(1, NU)] + [vp(i) for i in range(1, 4)]
    for peer in peers:
        pl.semaphore_signal(barrier, inc=1, device_id=peer, device_id_type=MESH)

    hbm = (pk_hbm, pv_hbm, rq_hbm, rk_hbm, pq_hbm, pdo_hbm, po_hbm, rdo_hbm, ro_hbm, rv_hbm)
    loads = [
        pltpu.make_async_copy(src, dst, lsem.at[i])
        for i, (src, dst) in enumerate(zip(hbm, (pk, pv, rq, rk, pq, pdo, po, rdo, ro, rv), strict=True))
    ]
    for load in loads:
        load.start()

    sem_no = {}

    def copy(key, src, dst, to):
        i = sem_no.setdefault(key, len(sem_no))
        return pltpu.make_async_remote_copy(
            src_ref=src, dst_ref=dst, send_sem=ssem.at[i], recv_sem=rsem.at[i],
            device_id=to, device_id_type=MESH,
        )

    def rows(off, n):
        return kvb.at[pl.ds(pl.multiple_of(off, S), n)]

    own_p = z * BLK + u * S
    own_q = HALF + u * BLK + z * S

    def g_pu(i):
        return copy(("gpu", i), rows(own_p, S), rows(own_p, S), up(i))

    def g_qz(i):
        return copy(("gqz", i), rows(own_q, S), rows(own_q, S), zp(i))

    def g_pz(right, s, k):
        b = rows(lax.rem(z + (NZ - s if right else s), NZ) * BLK + k * PIECE, PIECE)
        return copy(("gpz", right, s, k), b, b, zp(1 if right else NZ - 1))

    def g_qu(i):
        return copy(("gqu", i), rows(HALF + u * BLK, BLK), rows(HALF + u * BLK, BLK), up(i))

    def g_v(i):
        col = pl.multiple_of(lax.rem(kv + i, 4) * (H * D), H * D)
        return copy(
            ("gv", i),
            rdo.at[:, pl.ds(col, H * D)],
            arrived.at[pl.ds(pl.multiple_of(kv * 16, 16), 16)],
            vp(i),
        )

    def pieces(right, s):
        if s < NZ // 2 - 1:
            return range(SUBS)
        return range(SUBS // 2) if right else range(SUBS // 2, SUBS)

    def t_pz(right, t, k):
        part_of = pl.ds(k * SUM_PIECE, SUM_PIECE)
        if right:
            return copy(("tpr", t, k), s_r.at[t, part_of], r_r.at[t, part_of], zp(1))
        return copy(("tpl", t, k), s_l.at[t, part_of], r_l.at[t, part_of], zp(NZ - 1))

    def t_qu(i):
        return copy(("tqu", i), sq.at[i], rq_in.at[i], up(i))

    def t_pu(i):
        src = sp_out.at[pl.ds(pl.multiple_of(lax.rem(u + i, NU) * S, S), S)]
        return copy(("tpu", i), src, rp_in.at[i], up(i))

    def t_qz(i):
        src = sz_out.at[pl.ds(pl.multiple_of(lax.rem(z + i, NZ) * S, S), S)]
        return copy(("tqz", i), src, rz_in.at[i], zp(i))

    for load in loads:
        load.wait()
    for off, first_row in ((own_p, 0), (own_q, S)):
        kvb[pl.ds(pl.multiple_of(off, S), S), 0:D] = pk[first_row : first_row + S, :]
        kvb[pl.ds(pl.multiple_of(off, S), S), D : 2 * D] = pv[first_row : first_row + S, :]
    qs[0:ROWS] = by_head(pq)
    qs[ROWS : 2 * ROWS] = by_head(rq)
    prompt_cot = by_head(pdo)
    dos[0:ROWS] = prompt_cot
    dvec[:, 0:ROWS] = lane_dots(prompt_cot, by_head(po))
    dqt[...] = jnp.zeros_like(dqt)
    row_minus_col = lax.broadcasted_iota(jnp.int32, (R, ROWS), 0) - lax.rem(
        lax.broadcasted_iota(jnp.int32, (R, ROWS), 1), R
    )
    own_e = jnp.where(
        row_minus_col <= 0, jnp.exp2(dot(rk[...], qs[ROWS : 2 * ROWS], NT) * EXP2_SCALE), 0.0
    )
    eo[...] = own_e
    zs[:, 0:ROWS] = jnp.zeros((8, ROWS), F32)
    zs[:, ROWS : 2 * ROWS] = jnp.sum(own_e.reshape(R // 8, 8, ROWS), axis=0)
    pl.semaphore_wait(barrier, len(peers))

    for i in range(1, NU):
        g_pu(i).start()
    for i in (4, 3, 5, 2, 6, 1, 7):
        g_qz(i).start()
    for i in range(1, 4):
        g_v(i).start()
    arrived[pl.ds(pl.multiple_of(kv * 16, 16), 16), :] = rdo[:, pl.ds(pl.multiple_of(kv * (H * D), H * D), H * D)]
    for i in range(1, NU):
        g_pu(i).wait_recv()
    for k in range(SUBS):
        g_pz(True, 0, k).start()
        g_pz(False, 0, k).start()
    for i in range(1, NZ):
        g_qz(i).wait_recv()
    for i in range(1, NU):
        g_qu(i).start()

    def response_cotangents():
        for i in range(1, 4):
            g_v(i).wait_recv()
        tokens = lax.broadcasted_iota(jnp.int32, (R, R), 1)
        usable = (lmask[...] == 1) & (lax.broadcasted_iota(jnp.int32, (1, R), 1) < rlen[0])
        diagonal = lax.broadcasted_iota(jnp.int32, (R, R), 0) == tokens
        keep = jnp.sum(jnp.where(diagonal & usable, 1.0, 0.0), axis=1, keepdims=True)
        keep = jnp.broadcast_to(keep, (R, D)) > 0.5
        keep = jnp.concatenate([keep] * H, axis=0)
        cot = jnp.where(keep, by_head(arrived).astype(F32), 0.0).astype(BF)
        dos[ROWS : 2 * ROWS] = cot
        dvec[:, ROWS : 2 * ROWS] = lane_dots(cot, by_head(ro))

    def first(j, carry):
        for s in range(NZ // 2):

            @pl.when(j == (s + 1 if s < NZ // 2 - 1 else 7))
            def _():
                for k in range(SUBS):
                    for right in (True, False):
                        if k in pieces(right, s):
                            g_pz(right, s, k).wait_recv()
                            if s < NZ // 2 - 1 and k in pieces(right, s + 1):
                                g_pz(right, s + 1, k).start()
                if s == NZ // 2 - 1:
                    g_qu(NU - 1).wait_recv()

        @pl.when(j == NU // 2)
        def _():
            response_cotangents()

        for c in range(1, NU // 2):

            @pl.when(j == NU // 2 - 1 + c)
            def _():
                g_qu(2 * c - 1).wait_recv()
                g_qu(2 * c).wait_recv()

        q, opening, closing = j // 4, 1 - (j + 7) // 8, j // 7
        p1, p2 = 1 - q + closing, (1 - q) * (1 - opening)
        z1 = lax.rem(z + NZ - j * (1 - q) - 4 * closing, NZ)
        z2 = lax.rem(z + j, NZ)
        u1 = lax.rem(u + 2 * NU + 7 - 2 * j, NU)
        u2 = lax.rem(u + 2 * NU - q * (2 * j - 6) + closing, NU)
        off1 = p1 * (z1 * BLK) + (1 - p1) * (HALF + u1 * BLK)
        off2 = p2 * (z2 * BLK) + (1 - p2) * (HALF + u2 * BLK)
        off1, off2 = pl.multiple_of(off1, BLK), pl.multiple_of(off2, BLK)
        keys = jnp.concatenate([kvb[pl.ds(off1, 256), 0:D], kvb[pl.ds(off2, 256), 0:D]], axis=0)
        ex = jnp.exp2(dot(keys, qs[...], NT) * EXP2_SCALE)
        seen = []
        for p, zz, uu, top in ((p1, z1, u1, 0), (p2, z2, u2, BLK)):
            for g in range(8):
                in_p = (g // NY) * (NZ * NY) + zz * NY + g % NY
                in_q = (uu // NY) * (NZ * NY) + g * NY + lax.rem(uu, NY)
                limit = (w - (p * in_p + (1 - p) * in_q)) * R - (1 - p) * S
                block = ex[top + g * S : top + (g + 1) * S, 0:ROWS]
                seen.append(jnp.where(row_minus_col[0:S] <= limit, block, 0.0))
        seen = jnp.concatenate(seen, axis=0)
        rest = ex[:, ROWS : 2 * ROWS]
        for k, off in ((0, off1), (1, off2)):
            e[pl.ds(off, 256), 0:ROWS] = seen[k * 256 : (k + 1) * 256]
            e[pl.ds(off, 256), ROWS : 2 * ROWS] = rest[k * 256 : (k + 1) * 256]
        zs[:, 0:ROWS] += jnp.sum(seen.reshape(64, 8, ROWS), axis=0)
        zs[:, ROWS : 2 * ROWS] += jnp.sum(rest.reshape(64, 8, ROWS), axis=0)
        return carry

    lax.fori_loop(0, 8, first, 0)

    zs[...] = jnp.broadcast_to(1.0 / jnp.sum(zs[...], axis=0, keepdims=True), zs.shape)

    def chunk(j):
        t, mixed, odd = j // 2, j // 6, lax.rem(j, 2)
        p1, p2 = (1 - mixed) * (1 - odd) + mixed, (1 - mixed) * (1 - odd)
        z1, z2 = lax.rem(z + 4 - t - mixed * odd, NZ), lax.rem(z + 5 + t, NZ)
        u1, u2 = lax.rem(u + 2 * t + 1, NU), lax.rem(u + 2 * t + 2 - mixed * (1 - odd), NU)
        off1 = p1 * (z1 * BLK) + (1 - p1) * (HALF + u1 * BLK)
        off2 = p2 * (z2 * BLK) + (1 - p2) * (HALF + u2 * BLK)
        return pl.multiple_of(off1, BLK), pl.multiple_of(off2, BLK)

    def second(j, carry):
        off1, off2 = chunk(j)
        pair = jnp.concatenate([kvb[pl.ds(off1, 256), :], kvb[pl.ds(off2, 256), :]], axis=0)
        keys, values = pair[:, 0:D], pair[:, D : 2 * D]
        ex = jnp.concatenate([e[pl.ds(off1, 256), :], e[pl.ds(off2, 256), :]], axis=0)
        weights = ex * zs[0:1, :]
        part[:, D : 2 * D] = dot(weights.astype(BF), dos[...], NN)
        weight_grad = dot(values, dos[...], NT)
        score_grad = (weights * (weight_grad - dvec[0:1, :])).astype(BF)
        part[:, 0:D] = dot(score_grad, qs[...], NN)

        @pl.when(j < EARLY)
        def _():
            dqt[...] += dot(keys, score_grad, TN)

        @pl.when(j >= EARLY)
        def _():
            dss[pl.ds(pl.multiple_of((j - EARLY) * 512, 512), 512), :] = score_grad

        for t in range(3):

            @pl.when(j == 2 * t)
            def _():
                for k in range(SUMS):
                    piece = pl.ds(k * SUM_PIECE, SUM_PIECE)
                    right = part[k * SUM_PIECE : (k + 1) * SUM_PIECE, :]
                    left = part[BLK + k * SUM_PIECE : BLK + (k + 1) * SUM_PIECE, :]
                    if t > 0:
                        t_pz(True, t - 1, k).wait_recv()
                        right = right + r_r[t - 1, piece].astype(F32)
                    s_r[t, piece] = right.astype(BF)
                    t_pz(True, t, k).start()
                    if t > 0:
                        t_pz(False, t - 1, k).wait_recv()
                        left = left + r_l[t - 1, piece].astype(F32)
                    s_l[t, piece] = left.astype(BF)
                    t_pz(False, t, k).start()

            @pl.when(j == 2 * t + 1)
            def _():
                sq[2 * t + 1] = part[0:BLK, :].astype(BF)
                t_qu(2 * t + 1).start()
                sq[2 * t + 2] = part[BLK : 2 * BLK, :].astype(BF)
                t_qu(2 * t + 2).start()

        @pl.when(j == 6)
        def _():
            sq[NU - 1] = part[BLK : 2 * BLK, :].astype(BF)
            t_qu(NU - 1).start()
            acc_p[...] = part[0:BLK, :]

        @pl.when(j == 7)
        def _():
            for k in range(SUMS):
                piece = pl.ds(k * SUM_PIECE, SUM_PIECE)
                t_pz(True, 2, k).wait_recv()
                s_r[3, piece] = (acc_p[piece] + r_r[2, piece].astype(F32)).astype(BF)
                t_pz(True, 3, k).start()
            acc_p[...] = part[0:BLK, :]
            acc_q[...] = part[BLK : 2 * BLK, :]

        return carry

    lax.fori_loop(0, 8, second, 0)

    def late(i, carry):
        off1, off2 = chunk(i + EARLY)
        keys = jnp.concatenate([kvb[pl.ds(off1, 256), 0:D], kvb[pl.ds(off2, 256), 0:D]], axis=0)
        dqt[...] += dot(keys, dss[pl.ds(pl.multiple_of(i * 512, 512), 512), :], TN)

        @pl.when(i == 1)
        def _():
            total = acc_q[...]
            for k in range(1, NU):
                t_qu(k).wait_recv()
                total = total + rq_in[k].astype(F32)
            acc_q[...] = total
            sz_out[...] = total.astype(BF)
            for k in (4, 3, 5, 2, 6, 1, 7):
                t_qz(k).start()

        @pl.when(i == 4)
        def _():
            total = acc_p[...]
            for k in range(SUMS):
                t_pz(True, 3, k).wait_recv()
                t_pz(False, 2, k).wait_recv()
            total = total + r_r[3].astype(F32) + r_l[2].astype(F32)
            acc_p[...] = total
            sp_out[...] = total.astype(BF)
            for k in range(1, NU):
                t_pu(k).start()

        return carry

    lax.fori_loop(0, 8 - EARLY, late, 0)

    own_w = eo[...] * zs[0:1, ROWS : 2 * ROWS]
    kvg[3] = dot(own_w.astype(BF), dos[ROWS : 2 * ROWS], NN)
    own_g = dot(rv[...], dos[ROWS : 2 * ROWS], NT) - dvec[0:1, ROWS : 2 * ROWS]
    own_g = (own_w * own_g).astype(BF)
    kvg[2] = dot(own_g, qs[ROWS : 2 * ROWS], NN) * SCALE
    dqt[:, ROWS : 2 * ROWS] += dot(rk[...], own_g, TN)

    stores = [
        pltpu.make_async_copy(dq.at[0], dq_hbm.at[0], osem.at[0]),
        pltpu.make_async_copy(dq.at[1], dq_hbm.at[1], osem.at[1]),
        pltpu.make_async_copy(kvg, kvg_hbm, osem.at[2]),
    ]
    for which, first_col in ((0, 0), (1, ROWS)):
        for h in range(0, H, 2):
            block = dqt[:, first_col + h * R : first_col + (h + 2) * R].T * SCALE
            dq[which, :, h * D : (h + 1) * D] = block[0:R]
            dq[which, :, (h + 1) * D : (h + 2) * D] = block[R : 2 * R]
        stores[which].start()

    for i in range(1, NU):
        t_qz(i).wait_recv()
        t_pu(i).wait_recv()
    for acc, arrivals, place, first_row in ((acc_p, rp_in, u, 0), (acc_q, rz_in, z, S)):
        total = acc[pl.ds(pl.multiple_of(place * S, S), S), :]
        for i in range(1, NU):
            total = total + arrivals[i].astype(F32)
        kvg[0, first_row : first_row + S, :] = total[:, 0:D] * SCALE
        kvg[1, first_row : first_row + S, :] = total[:, D : 2 * D]
    stores[2].start()

    for i in range(1, NU):
        for sent in (g_pu, g_qz, g_qu, t_qu, t_pu, t_qz):
            sent(i).wait_send()
    for i in range(1, 4):
        g_v(i).wait_send()
    for right in (True, False):
        for s in range(NZ // 2):
            for k in pieces(right, s):
                g_pz(right, s, k).wait_send()
            if right or s < 3:
                for k in range(SUMS):
                    t_pz(right, s, k).wait_send()
    for store in stores:
        store.wait()


def hand_out(dq, kvg, pdq, pdk, pdv, rdq, rdk, rdv):
    pdq[...] = dq[0]
    rdq[...] = dq[1]
    for i, out in enumerate((pdk, pdv, rdk, rdv)):
        out[...] = kvg[i]


def local(
    prompt_q, prompt_k, prompt_v, prompt_out, prompt_dout,
    resp_q, resp_k, resp_v, resp_out, resp_dout, resp_len, loss_mask,
):
    vmem = pl.BlockSpec(memory_space=pltpu.VMEM)
    smem = pl.BlockSpec(memory_space=pltpu.SMEM)
    anywhere = pl.BlockSpec(memory_space=pl.ANY)
    wide_out = jax.ShapeDtypeStruct((R, H * D), F32)
    head_out = jax.ShapeDtypeStruct((R, D), F32)
    V = pltpu.VMEM
    wide_in, head_in = V((R, H * D), BF), V((R, D), BF)
    sums = pl.pallas_call(
        kernel,
        out_shape=[jax.ShapeDtypeStruct((2, R, H * D), F32), jax.ShapeDtypeStruct((4, R, D), F32)],
        in_specs=[anywhere] * 10 + [smem, vmem],
        out_specs=[anywhere] * 2,
        scratch_shapes=[
            wide_in, head_in, head_in, wide_in, wide_in,
            wide_in, head_in, head_in, wide_in, V((16, 4 * H * D), BF),
            V((2, R, H * D), F32),
            V((4, R, D), F32),
            V((2 * HALF, 2 * D), BF),
            V((2 * ROWS, D), BF),
            V((2 * ROWS, D), BF),
            V((R, H * D), BF),
            V((2 * HALF, 2 * ROWS), F32),
            V((R, ROWS), F32),
            V((2 * HALF - EARLY * 512, 2 * ROWS), BF),
            V((8, 2 * ROWS), F32),
            V((8, 2 * ROWS), F32),
            V((D, 2 * ROWS), F32),
            V((512, 2 * D), F32),
            V((BLK, 2 * D), F32),
            V((BLK, 2 * D), F32),
            V((4, BLK, 2 * D), BF),
            V((3, BLK, 2 * D), BF),
            V((4, BLK, 2 * D), BF),
            V((3, BLK, 2 * D), BF),
            V((NU, BLK, 2 * D), BF),
            V((NU, BLK, 2 * D), BF),
            V((BLK, 2 * D), BF),
            V((NU, S, 2 * D), BF),
            V((BLK, 2 * D), BF),
            V((NZ, S, 2 * D), BF),
            pltpu.SemaphoreType.DMA((COPIES,)),
            pltpu.SemaphoreType.DMA((COPIES,)),
            pltpu.SemaphoreType.DMA((10,)),
            pltpu.SemaphoreType.DMA((3,)),
        ],
        compiler_params=pltpu.CompilerParams(
            collective_id=0, has_side_effects=True, vmem_limit_bytes=63 * 2**20
        ),
    )(
        prompt_q, prompt_k, prompt_v, prompt_out, prompt_dout,
        resp_q, resp_k, resp_v, resp_out, resp_dout, resp_len, loss_mask.reshape(1, R),
    )
    return pl.pallas_call(
        hand_out,
        out_shape=[wide_out, head_out, head_out, wide_out, head_out, head_out],
        in_specs=[vmem] * 2,
        out_specs=[vmem] * 6,
    )(*sums)


def solution(mesh):
    grid = P("wide", "kv")
    return jax.shard_map(
        local,
        mesh=mesh,
        in_specs=(grid,) * 9 + (P(("wide", "kv"), None), P("wide"), P("wide")),
        out_specs=(grid,) * 6,
        check_vma=False,
    )
```

time: 80.2 us -> 66.4 us (0.83)
  Pallas kernels: 72.8 us -> 65 us
  local copies, waits for them, and re-layouts: 5.5 us -> 0 us
    pallas_call x1 -> x2, Pallas kernels: 72.8 us -> 65 us  [the longest x1 62.7 us: local(): pl.pallas_call(kernel, out_shape=[jax.ShapeDtypeStruct((2, R, H * D), F32...]
    unnamed x16 -> x0, local copies, waits for them, and re-layouts: 5.5 us -> none
where the time goes in v2:
time: 66.4 us; the launch traced here: 66.2 us
  Pallas kernels  65 us (98%)
  between operations  1.29 us (2%)
    pallas_call x1, Pallas kernels, local(): pl.pallas_call(kernel, out_shape=[jax.ShapeDtypeStruct((2, R, H * D), F32...  62.7 us
    pallas_call x1, Pallas kernels, local(): pl.pallas_call(hand_out, out_shape=[wide_out, head_out, head_out, wide_ou...  2.26 us

profile of v2, /device:TPU:16, one launch (start us, length us, event | category | flops | bytes accessed | tf_op | source)
XLA Modules:
  0.0 66.2 jit_solution(566119802074853192)
XLA Ops:
  1.3 62.7 %shard_map.163 = (f32[2,64,2048]{2,1,0:T(8,128)}, f32[4,64,128]{2,1,0:T(8,128)}) custom-call(bf16[64,2048]{1,0:T(8,128)(2,1)} %pq_hbm.1, bf16[64,128]{1,0:T(8,128)(2,1)} %pk_hbm.1, bf16[64,128]{1,0:T(8,128)(2,1)} %pv_hbm.1, bf16[64,2048]{1,0:T(8,128)(2,1)} %po_hbm.1, bf16[64,2048]{1,0:T(8,128)(2,1)} %pdo_hbm.1, bf16[64,2048]{1,0:T(8,128)(2,1)} %rq_hbm.1, ...), custom_call_target="tpu_custom_call" | custom-call | tf_op jit(solution)/shard_map/pallas_call | solution.py:427
  64.0 2.3 %shard_map.164 = (f32[64,2048]{1,0:T(8,128)}, f32[64,128]{1,0:T(8,128)}, f32[64,128]{1,0:T(8,128)}, f32[64,2048]{1,0:T(8,128)}, f32[64,128]{1,0:T(8,128)}, /*index=5*/f32[64,128]{1,0:T(8,128)}) custom-call(f32[2,64,2048]{2,1,0:T(8,128)} %get-tuple-element.8.dq, f32[4,64,128]{2,1,0:T(8,128)} %get-tuple-element.9.kvg), custom_call_target="tpu_custom_call" | custom-call | tf_op jit(solution)/shard_map/pallas_call | solution.py:472

commit v3 on v2

--- a/solution.py
+++ b/solution.py
@@ -22,7 +22,7 @@
 EXP2_SCALE = math.log2(math.e) / math.sqrt(D)
 HALF = NU * NZ * S
 BLK = NU * S
-SUBS = 4
+SUBS = NX
 PIECE = BLK // SUBS
 SUMS = 2
 SUM_PIECE = BLK // SUMS
@@ -30,7 +30,6 @@
 NT = (((1,), (1,)), ((), ()))
 TN = (((0,), (0,)), ((), ()))
 COPIES = 87
-EARLY = 2
 
 
 def dot(a, b, dims):
@@ -52,8 +51,8 @@
 def kernel(
     pq_hbm, pk_hbm, pv_hbm, po_hbm, pdo_hbm, rq_hbm, rk_hbm, rv_hbm, ro_hbm, rdo_hbm, rlen, lmask,
     dq_hbm, kvg_hbm,
-    pq, pk, pv, po, pdo, rq, rk, rv, ro, rdo, dq, kvg,
-    kvb, qs, dos, arrived, e, eo, dss, zs, dvec, dqt, part, acc_p, acc_q,
+    pk, pv, rk, rv, rdo, dq, kvg,
+    kvb, qs, dos, e, eo, dss, zs, dvec, dqt, part, acc_p, acc_q,
     s_r, s_l, r_r, r_l, sq, rq_in, sp_out, rp_in, sz_out, rz_in,
     ssem, rsem, lsem, osem,
 ):
@@ -64,8 +63,14 @@
     def dev(uu, zz, vv):
         return (((uu // NY) * NZ + zz) * NY + lax.rem(uu, NY), vv)
 
+    def u_to(i):
+        return lax.rem(x + i // NY, NX) * NY + lax.rem(y + lax.rem(i, NY), NY)
+
+    def u_from(i):
+        return lax.rem(x + NX - i // NY, NX) * NY + lax.rem(y + lax.rem(i, NY), NY)
+
     def up(i):
-        return dev(lax.rem(u + i, NU), z, kv)
+        return dev(u_to(i), z, kv)
 
     def zp(i):
         return dev(u, lax.rem(z + i, NZ), kv)
@@ -78,6 +83,7 @@
     for peer in peers:
         pl.semaphore_signal(barrier, inc=1, device_id=peer, device_id_type=MESH)
 
+    pq, po, pdo, rq, ro, arrived = (dss.at[pl.ds(i * R, R)] for i in range(6))
     hbm = (pk_hbm, pv_hbm, rq_hbm, rk_hbm, pq_hbm, pdo_hbm, po_hbm, rdo_hbm, ro_hbm, rv_hbm)
     loads = [
         pltpu.make_async_copy(src, dst, lsem.at[i])
@@ -108,7 +114,8 @@
         return copy(("gqz", i), rows(own_q, S), rows(own_q, S), zp(i))
 
     def g_pz(right, s, k):
-        b = rows(lax.rem(z + (NZ - s if right else s), NZ) * BLK + k * PIECE, PIECE)
+        at = lax.rem(x + NX - k, NX)
+        b = rows(lax.rem(z + (NZ - s if right else s), NZ) * BLK + at * PIECE, PIECE)
         return copy(("gpz", right, s, k), b, b, zp(1 if right else NZ - 1))
 
     def g_qu(i):
@@ -138,7 +145,7 @@
         return copy(("tqu", i), sq.at[i], rq_in.at[i], up(i))
 
     def t_pu(i):
-        src = sp_out.at[pl.ds(pl.multiple_of(lax.rem(u + i, NU) * S, S), S)]
+        src = sp_out.at[pl.ds(pl.multiple_of(u_to(i) * S, S), S)]
         return copy(("tpu", i), src, rp_in.at[i], up(i))
 
     def t_qz(i):
@@ -174,9 +181,10 @@
     for i in range(1, 4):
         g_v(i).start()
     arrived[pl.ds(pl.multiple_of(kv * 16, 16), 16), :] = rdo[:, pl.ds(pl.multiple_of(kv * (H * D), H * D), H * D)]
-    for i in range(1, NU):
-        g_pu(i).wait_recv()
     for k in range(SUBS):
+        for i in range(NY * k, NY * (k + 1)):
+            if i > 0:
+                g_pu(i).wait_recv()
         g_pz(True, 0, k).start()
         g_pz(False, 0, k).start()
     for i in range(1, NZ):
@@ -188,7 +196,7 @@
         for i in range(1, 4):
             g_v(i).wait_recv()
         tokens = lax.broadcasted_iota(jnp.int32, (R, R), 1)
-        usable = (lmask[...] == 1) & (lax.broadcasted_iota(jnp.int32, (1, R), 1) < rlen[0])
+        usable = (lmask[...] == 1) & (lax.broadcasted_iota(jnp.int32, (1, R), 1) < rlen[...])
         diagonal = lax.broadcasted_iota(jnp.int32, (R, R), 0) == tokens
         keep = jnp.sum(jnp.where(diagonal & usable, 1.0, 0.0), axis=1, keepdims=True)
         keep = jnp.broadcast_to(keep, (R, D)) > 0.5
@@ -226,8 +234,8 @@
         p1, p2 = 1 - q + closing, (1 - q) * (1 - opening)
         z1 = lax.rem(z + NZ - j * (1 - q) - 4 * closing, NZ)
         z2 = lax.rem(z + j, NZ)
-        u1 = lax.rem(u + 2 * NU + 7 - 2 * j, NU)
-        u2 = lax.rem(u + 2 * NU - q * (2 * j - 6) + closing, NU)
+        u1 = u_from(lax.rem(2 * NU + 2 * j - 7, NU))
+        u2 = u_from(q * (2 * j - 6) - closing)
         off1 = p1 * (z1 * BLK) + (1 - p1) * (HALF + u1 * BLK)
         off2 = p2 * (z2 * BLK) + (1 - p2) * (HALF + u2 * BLK)
         off1, off2 = pl.multiple_of(off1, BLK), pl.multiple_of(off2, BLK)
@@ -258,29 +266,20 @@
         t, mixed, odd = j // 2, j // 6, lax.rem(j, 2)
         p1, p2 = (1 - mixed) * (1 - odd) + mixed, (1 - mixed) * (1 - odd)
         z1, z2 = lax.rem(z + 4 - t - mixed * odd, NZ), lax.rem(z + 5 + t, NZ)
-        u1, u2 = lax.rem(u + 2 * t + 1, NU), lax.rem(u + 2 * t + 2 - mixed * (1 - odd), NU)
+        u1, u2 = u_to(2 * t + 1), u_to(lax.rem(2 * t + 2 - mixed * (1 - odd), NU))
         off1 = p1 * (z1 * BLK) + (1 - p1) * (HALF + u1 * BLK)
         off2 = p2 * (z2 * BLK) + (1 - p2) * (HALF + u2 * BLK)
         return pl.multiple_of(off1, BLK), pl.multiple_of(off2, BLK)
 
     def second(j, carry):
         off1, off2 = chunk(j)
-        pair = jnp.concatenate([kvb[pl.ds(off1, 256), :], kvb[pl.ds(off2, 256), :]], axis=0)
-        keys, values = pair[:, 0:D], pair[:, D : 2 * D]
-        ex = jnp.concatenate([e[pl.ds(off1, 256), :], e[pl.ds(off2, 256), :]], axis=0)
-        weights = ex * zs[0:1, :]
-        part[:, D : 2 * D] = dot(weights.astype(BF), dos[...], NN)
-        weight_grad = dot(values, dos[...], NT)
-        score_grad = (weights * (weight_grad - dvec[0:1, :])).astype(BF)
-        part[:, 0:D] = dot(score_grad, qs[...], NN)
-
-        @pl.when(j < EARLY)
-        def _():
-            dqt[...] += dot(keys, score_grad, TN)
-
-        @pl.when(j >= EARLY)
-        def _():
-            dss[pl.ds(pl.multiple_of((j - EARLY) * 512, 512), 512), :] = score_grad
+        for off, top in ((off1, 0), (off2, BLK)):
+            weights = e[pl.ds(off, BLK), :] * zs[0:1, :]
+            part[top : top + BLK, D : 2 * D] = dot(weights.astype(BF), dos[...], NN)
+            weight_grad = dot(kvb[pl.ds(off, BLK), D : 2 * D], dos[...], NT)
+            score_grad = (weights * (weight_grad - dvec[0:1, :])).astype(BF)
+            dss[pl.ds(pl.multiple_of(j * (2 * BLK), 2 * BLK) + top, BLK), :] = score_grad
+            part[top : top + BLK, 0:D] = dot(score_grad, qs[...], NN)
 
         for t in range(3):
 
@@ -312,15 +311,14 @@
         def _():
             sq[NU - 1] = part[BLK : 2 * BLK, :].astype(BF)
             t_qu(NU - 1).start()
-            acc_p[...] = part[0:BLK, :]
-
-        @pl.when(j == 7)
-        def _():
             for k in range(SUMS):
                 piece = pl.ds(k * SUM_PIECE, SUM_PIECE)
                 t_pz(True, 2, k).wait_recv()
-                s_r[3, piece] = (acc_p[piece] + r_r[2, piece].astype(F32)).astype(BF)
+                s_r[3, piece] = (part[k * SUM_PIECE : (k + 1) * SUM_PIECE, :] + r_r[2, piece].astype(F32)).astype(BF)
                 t_pz(True, 3, k).start()
+
+        @pl.when(j == 7)
+        def _():
             acc_p[...] = part[0:BLK, :]
             acc_q[...] = part[BLK : 2 * BLK, :]
 
@@ -329,7 +327,7 @@
     lax.fori_loop(0, 8, second, 0)
 
     def late(i, carry):
-        off1, off2 = chunk(i + EARLY)
+        off1, off2 = chunk(i)
         keys = jnp.concatenate([kvb[pl.ds(off1, 256), 0:D], kvb[pl.ds(off2, 256), 0:D]], axis=0)
         dqt[...] += dot(keys, dss[pl.ds(pl.multiple_of(i * 512, 512), 512), :], TN)
 
@@ -344,7 +342,7 @@
             for k in (4, 3, 5, 2, 6, 1, 7):
                 t_qz(k).start()
 
-        @pl.when(i == 4)
+        @pl.when(i == 2)
         def _():
             total = acc_p[...]
             for k in range(SUMS):
@@ -358,7 +356,7 @@
 
         return carry
 
-    lax.fori_loop(0, 8 - EARLY, late, 0)
+    lax.fori_loop(0, 8, late, 0)
 
     own_w = eo[...] * zs[0:1, ROWS : 2 * ROWS]
     kvg[3] = dot(own_w.astype(BF), dos[ROWS : 2 * ROWS], NN)
@@ -418,29 +416,26 @@
     resp_q, resp_k, resp_v, resp_out, resp_dout, resp_len, loss_mask,
 ):
     vmem = pl.BlockSpec(memory_space=pltpu.VMEM)
-    smem = pl.BlockSpec(memory_space=pltpu.SMEM)
     anywhere = pl.BlockSpec(memory_space=pl.ANY)
     wide_out = jax.ShapeDtypeStruct((R, H * D), F32)
     head_out = jax.ShapeDtypeStruct((R, D), F32)
     V = pltpu.VMEM
-    wide_in, head_in = V((R, H * D), BF), V((R, D), BF)
+    head_in = V((R, D), BF)
     sums = pl.pallas_call(
         kernel,
         out_shape=[jax.ShapeDtypeStruct((2, R, H * D), F32), jax.ShapeDtypeStruct((4, R, D), F32)],
-        in_specs=[anywhere] * 10 + [smem, vmem],
+        in_specs=[anywhere] * 10 + [vmem] * 2,
         out_specs=[anywhere] * 2,
         scratch_shapes=[
-            wide_in, head_in, head_in, wide_in, wide_in,
-            wide_in, head_in, head_in, wide_in, V((16, 4 * H * D), BF),
+            head_in, head_in, head_in, head_in, V((16, 4 * H * D), BF),
             V((2, R, H * D), F32),
             V((4, R, D), F32),
             V((2 * HALF, 2 * D), BF),
             V((2 * ROWS, D), BF),
             V((2 * ROWS, D), BF),
-            V((R, H * D), BF),
             V((2 * HALF, 2 * ROWS), F32),
             V((R, ROWS), F32),
-            V((2 * HALF - EARLY * 512, 2 * ROWS), BF),
+            V((2 * HALF, 2 * ROWS), BF),
             V((8, 2 * ROWS), F32),
             V((8, 2 * ROWS), F32),
             V((D, 2 * ROWS), F32),
@@ -463,11 +458,11 @@
             pltpu.SemaphoreType.DMA((3,)),
         ],
         compiler_params=pltpu.CompilerParams(
-            collective_id=0, has_side_effects=True, vmem_limit_bytes=63 * 2**20
+            collective_id=0, has_side_effects=True, vmem_limit_bytes=127 * 2**19
         ),
     )(
         prompt_q, prompt_k, prompt_v, prompt_out, prompt_dout,
-        resp_q, resp_k, resp_v, resp_out, resp_dout, resp_len, loss_mask.reshape(1, R),
+        resp_q, resp_k, resp_v, resp_out, resp_dout, resp_len.reshape(1, 1), loss_mask.reshape(1, R),
     )
     return pl.pallas_call(
         hand_out,

time: 66.4 us -> 63.6 us (0.958)
  Pallas kernels: 65 us -> 62 us
    pallas_call x1, Pallas kernels: 62.7 us -> 59.7 us  [local(): pl.pallas_call(kernel, out_shape=[jax.ShapeDtypeStruct((2, R, H * D), F32...]
where the time goes in v3:
time: 63.6 us; the launch traced here: 63.3 us
  Pallas kernels  62 us (97%)
  between operations  1.29 us (2%)
    pallas_call x1, Pallas kernels, local(): pl.pallas_call(kernel, out_shape=[jax.ShapeDtypeStruct((2, R, H * D), F32...  59.7 us
    pallas_call x1, Pallas kernels, local(): pl.pallas_call(hand_out, out_shape=[wide_out, head_out, head_out, wide_ou...  2.26 us

profile of v3, /device:TPU:16, one launch (start us, length us, event | category | flops | bytes accessed | tf_op | source)
XLA Modules:
  0.0 63.3 jit_solution(16767319676807522157)
XLA Ops:
  1.3 59.7 %shard_map.163 = (f32[2,64,2048]{2,1,0:T(8,128)}, f32[4,64,128]{2,1,0:T(8,128)}) custom-call(bf16[64,2048]{1,0:T(8,128)(2,1)} %pq_hbm.1, bf16[64,128]{1,0:T(8,128)(2,1)} %pk_hbm.1, bf16[64,128]{1,0:T(8,128)(2,1)} %pv_hbm.1, bf16[64,2048]{1,0:T(8,128)(2,1)} %po_hbm.1, bf16[64,2048]{1,0:T(8,128)(2,1)} %pdo_hbm.1, bf16[64,2048]{1,0:T(8,128)(2,1)} %rq_hbm.1, ...), custom_call_target="tpu_custom_call" | custom-call | tf_op jit(solution)/shard_map/pallas_call | solution.py:424
  61.0 2.3 %shard_map.164 = (f32[64,2048]{1,0:T(8,128)}, f32[64,128]{1,0:T(8,128)}, f32[64,128]{1,0:T(8,128)}, f32[64,2048]{1,0:T(8,128)}, f32[64,128]{1,0:T(8,128)}, /*index=5*/f32[64,128]{1,0:T(8,128)}) custom-call(f32[2,64,2048]{2,1,0:T(8,128)} %get-tuple-element.8.dq, f32[4,64,128]{2,1,0:T(8,128)} %get-tuple-element.9.kvg), custom_call_target="tpu_custom_call" | custom-call | tf_op jit(solution)/shard_map/pallas_call | solution.py:467

commit v4 on v3

--- a/solution.py
+++ b/solution.py
@@ -263,10 +263,11 @@
     zs[...] = jnp.broadcast_to(1.0 / jnp.sum(zs[...], axis=0, keepdims=True), zs.shape)
 
     def chunk(j):
-        t, mixed, odd = j // 2, j // 6, lax.rem(j, 2)
-        p1, p2 = (1 - mixed) * (1 - odd) + mixed, (1 - mixed) * (1 - odd)
-        z1, z2 = lax.rem(z + 4 - t - mixed * odd, NZ), lax.rem(z + 5 + t, NZ)
-        u1, u2 = u_to(2 * t + 1), u_to(lax.rem(2 * t + 2 - mixed * (1 - odd), NU))
+        odd, from_5, from_6, last = lax.rem(j, 2), j // 5, j // 6, j // 7
+        p1 = 1 - odd + last
+        p2 = (1 - odd) * (1 - (j // 4) * (1 - from_5))
+        z1, z2 = lax.rem(z + 4 - j // 2 - last, NZ), lax.rem(z + 5 + j // 2 - from_6, NZ)
+        u1, u2 = u_to(8 - j - from_5), u_to(7 - j - from_5 + last)
         off1 = p1 * (z1 * BLK) + (1 - p1) * (HALF + u1 * BLK)
         off2 = p2 * (z2 * BLK) + (1 - p2) * (HALF + u2 * BLK)
         return pl.multiple_of(off1, BLK), pl.multiple_of(off2, BLK)
@@ -281,41 +282,55 @@
             dss[pl.ds(pl.multiple_of(j * (2 * BLK), 2 * BLK) + top, BLK), :] = score_grad
             part[top : top + BLK, 0:D] = dot(score_grad, qs[...], NN)
 
-        for t in range(3):
-
-            @pl.when(j == 2 * t)
-            def _():
-                for k in range(SUMS):
-                    piece = pl.ds(k * SUM_PIECE, SUM_PIECE)
-                    right = part[k * SUM_PIECE : (k + 1) * SUM_PIECE, :]
-                    left = part[BLK + k * SUM_PIECE : BLK + (k + 1) * SUM_PIECE, :]
-                    if t > 0:
-                        t_pz(True, t - 1, k).wait_recv()
-                        right = right + r_r[t - 1, piece].astype(F32)
-                    s_r[t, piece] = right.astype(BF)
-                    t_pz(True, t, k).start()
-                    if t > 0:
-                        t_pz(False, t - 1, k).wait_recv()
-                        left = left + r_l[t - 1, piece].astype(F32)
-                    s_l[t, piece] = left.astype(BF)
-                    t_pz(False, t, k).start()
-
-            @pl.when(j == 2 * t + 1)
-            def _():
-                sq[2 * t + 1] = part[0:BLK, :].astype(BF)
-                t_qu(2 * t + 1).start()
-                sq[2 * t + 2] = part[BLK : 2 * BLK, :].astype(BF)
-                t_qu(2 * t + 2).start()
-
-        @pl.when(j == 6)
-        def _():
-            sq[NU - 1] = part[BLK : 2 * BLK, :].astype(BF)
-            t_qu(NU - 1).start()
+        def send_p(right, t, top):
+            sent, arrived_sum = (s_r, r_r) if right else (s_l, r_l)
             for k in range(SUMS):
                 piece = pl.ds(k * SUM_PIECE, SUM_PIECE)
-                t_pz(True, 2, k).wait_recv()
-                s_r[3, piece] = (part[k * SUM_PIECE : (k + 1) * SUM_PIECE, :] + r_r[2, piece].astype(F32)).astype(BF)
-                t_pz(True, 3, k).start()
+                value = part[top + k * SUM_PIECE : top + (k + 1) * SUM_PIECE, :]
+                if t > 0:
+                    t_pz(right, t - 1, k).wait_recv()
+                    value = value + arrived_sum[t - 1, piece].astype(F32)
+                sent[t, piece] = value.astype(BF)
+                t_pz(right, t, k).start()
+
+        def send_q(i, top):
+            sq[i] = part[top : top + BLK, :].astype(BF)
+            t_qu(i).start()
+
+        @pl.when(j == 0)
+        def _():
+            send_p(True, 0, 0)
+            send_p(False, 0, BLK)
+
+        @pl.when(j == 1)
+        def _():
+            send_q(7, 0)
+            send_q(6, BLK)
+
+        @pl.when(j == 2)
+        def _():
+            send_p(True, 1, 0)
+            send_p(False, 1, BLK)
+
+        @pl.when(j == 3)
+        def _():
+            send_q(5, 0)
+            send_q(4, BLK)
+
+        @pl.when(j == 4)
+        def _():
+            send_q(3, BLK)
+            send_p(True, 2, 0)
+
+        @pl.when(j == 5)
+        def _():
+            send_q(2, 0)
+            send_q(1, BLK)
+
+        @pl.when(j == 6)
+        def _():
+            send_p(False, 2, BLK)
+            send_p(True, 3, 0)
 
         @pl.when(j == 7)
         def _():

time: 63.6 us -> 62.5 us (0.983)
  the two profiles are of different devices: /device:TPU:16 before, /device:TPU:1 now
where the time goes in v4:
time: 62.5 us; the launch traced here: 62.3 us
  Pallas kernels  61 us (98%)
  between operations  1.29 us (2%)
    pallas_call x1, Pallas kernels, local(): pl.pallas_call(kernel, out_shape=[jax.ShapeDtypeStruct((2, R, H * D), F32...  58.7 us
    pallas_call x1, Pallas kernels, local(): pl.pallas_call(hand_out, out_shape=[wide_out, head_out, head_out, wide_ou...  2.26 us

profile of v4, /device:TPU:1, one launch (start us, length us, event | category | flops | bytes accessed | tf_op | source)
XLA Modules:
  0.0 62.3 jit_solution(5895114306553507081)
XLA Ops:
  1.3 58.7 %shard_map.163 = (f32[2,64,2048]{2,1,0:T(8,128)}, f32[4,64,128]{2,1,0:T(8,128)}) custom-call(bf16[64,2048]{1,0:T(8,128)(2,1)} %pq_hbm.1, bf16[64,128]{1,0:T(8,128)(2,1)} %pk_hbm.1, bf16[64,128]{1,0:T(8,128)(2,1)} %pv_hbm.1, bf16[64,2048]{1,0:T(8,128)(2,1)} %po_hbm.1, bf16[64,2048]{1,0:T(8,128)(2,1)} %pdo_hbm.1, bf16[64,2048]{1,0:T(8,128)(2,1)} %rq_hbm.1, ...), custom_call_target="tpu_custom_call" | custom-call | tf_op jit(solution)/shard_map/pallas_call | solution.py:439
  60.0 2.3 %shard_map.164 = (f32[64,2048]{1,0:T(8,128)}, f32[64,128]{1,0:T(8,128)}, f32[64,128]{1,0:T(8,128)}, f32[64,2048]{1,0:T(8,128)}, f32[64,128]{1,0:T(8,128)}, /*index=5*/f32[64,128]{1,0:T(8,128)}) custom-call(f32[2,64,2048]{2,1,0:T(8,128)} %get-tuple-element.8.dq, f32[4,64,128]{2,1,0:T(8,128)} %get-tuple-element.9.kvg), custom_call_target="tpu_custom_call" | custom-call | tf_op jit(solution)/shard_map/pallas_call | solution.py:482

commit v5 on v4

--- a/solution.py
+++ b/solution.py
@@ -29,7 +29,7 @@
 NN = (((1,), (0,)), ((), ()))
 NT = (((1,), (1,)), ((), ()))
 TN = (((0,), (0,)), ((), ()))
-COPIES = 87
+COPIES = 69
 
 
 def dot(a, b, dims):
@@ -95,11 +95,25 @@
     sem_no = {}
 
     def copy(key, src, dst, to):
+        if key[0] in ("gqz", "tpu", "tqz"):
+            key = key[0]
         i = sem_no.setdefault(key, len(sem_no))
         return pltpu.make_async_remote_copy(
             src_ref=src, dst_ref=dst, send_sem=ssem.at[i], recv_sem=rsem.at[i],
             device_id=to, device_id_type=MESH,
         )
+
+    def seven(key, ref):
+        return copy((key,), ref, ref, zp(1))
+
+    def g_qz_all():
+        return seven("gqz", kvb.at[pl.ds(0, (NZ - 1) * S)])
+
+    def t_pu_all():
+        return seven("tpu", rp_in.at[pl.ds(1, NU - 1)])
+
+    def t_qz_all():
+        return seven("tqz", rz_in.at[pl.ds(1, NZ - 1)])
 
     def rows(off, n):
         return kvb.at[pl.ds(pl.multiple_of(off, S), n)]
@@ -187,8 +201,7 @@
                 g_pu(i).wait_recv()
         g_pz(True, 0, k).start()
         g_pz(False, 0, k).start()
-    for i in range(1, NZ):
-        g_qz(i).wait_recv()
+    g_qz_all().wait_recv()
     for i in range(1, NU):
         g_qu(i).start()
 
@@ -392,9 +405,8 @@
             dq[which, :, (h + 1) * D : (h + 2) * D] = block[R : 2 * R]
         stores[which].start()
 
-    for i in range(1, NU):
-        t_qz(i).wait_recv()
-        t_pu(i).wait_recv()
+    t_qz_all().wait_recv()
+    t_pu_all().wait_recv()
     for acc, arrivals, place, first_row in ((acc_p, rp_in, u, 0), (acc_q, rz_in, z, S)):
         total = acc[pl.ds(pl.multiple_of(place * S, S), S), :]
         for i in range(1, NU):
@@ -404,8 +416,10 @@
     stores[2].start()
 
     for i in range(1, NU):
-        for sent in (g_pu, g_qz, g_qu, t_qu, t_pu, t_qz):
+        for sent in (g_pu, g_qu, t_qu):
             sent(i).wait_send()
+    for every in (g_qz_all, t_pu_all, t_qz_all):
+        every().wait_send()
     for i in range(1, 4):
         g_v(i).wait_send()
     for right in (True, False):
@@ -419,11 +433,25 @@
         store.wait()
 
 
-def hand_out(dq, kvg, pdq, pdk, pdv, rdq, rdk, rdv):
-    pdq[...] = dq[0]
-    rdq[...] = dq[1]
-    for i, out in enumerate((pdk, pdv, rdk, rdv)):
-        out[...] = kvg[i]
+def hand_out(dq_hbm, kvg_hbm, pdq, pdk, pdv, rdq, rdk, rdv, dq, kvg, isem, osem):
+    loads = [
+        pltpu.make_async_copy(dq_hbm.at[0], dq.at[0], isem.at[0]),
+        pltpu.make_async_copy(dq_hbm.at[1], dq.at[1], isem.at[1]),
+        pltpu.make_async_copy(kvg_hbm, kvg, isem.at[2]),
+    ]
+    for load in loads:
+        load.start()
+    stores = [pltpu.make_async_copy(dq.at[i], out, osem.at[i]) for i, out in enumerate((pdq, rdq))]
+    stores += [pltpu.make_async_copy(kvg.at[i], out, osem.at[2 + i]) for i, out in enumerate((pdk, pdv, rdk, rdv))]
+    loads[0].wait()
+    stores[0].start()
+    loads[1].wait()
+    stores[1].start()
+    loads[2].wait()
+    for store in stores[2:]:
+        store.start()
+    for store in stores:
+        store.wait()
 
 
 def local(
@@ -482,8 +510,14 @@
     return pl.pallas_call(
         hand_out,
         out_shape=[wide_out, head_out, head_out, wide_out, head_out, head_out],
-        in_specs=[vmem] * 2,
-        out_specs=[vmem] * 6,
+        in_specs=[anywhere] * 2,
+        out_specs=[anywhere] * 6,
+        scratch_shapes=[
+            V((2, R, H * D), F32),
+            V((4, R, D), F32),
+            pltpu.SemaphoreType.DMA((3,)),
+            pltpu.SemaphoreType.DMA((6,)),
+        ],
     )(*sums)
 
 

time: 62.5 us -> 62.3 us (level)
  no operation moved by 1% of the time
where the time goes in v5:
time: 62.3 us; the launch traced here: 62.1 us
  Pallas kernels  60.8 us (98%)
  between operations  1.29 us (2%)
    pallas_call x1, Pallas kernels, local(): pl.pallas_call(kernel, out_shape=[jax.ShapeDtypeStruct((2, R, H * D), F32...  58.7 us
    pallas_call x1, Pallas kernels, local(): pl.pallas_call(hand_out, out_shape=[wide_out, head_out, head_out, wide_ou...  2.11 us

profile of v5, /device:TPU:1, one launch (start us, length us, event | category | flops | bytes accessed | tf_op | source)
XLA Modules:
  0.0 62.1 jit_solution(11853777637389396415)
XLA Ops:
  1.3 58.7 %shard_map.163 = (f32[2,64,2048]{2,1,0:T(8,128)}, f32[4,64,128]{2,1,0:T(8,128)}) custom-call(bf16[64,2048]{1,0:T(8,128)(2,1)} %pq_hbm.1, bf16[64,128]{1,0:T(8,128)(2,1)} %pk_hbm.1, bf16[64,128]{1,0:T(8,128)(2,1)} %pv_hbm.1, bf16[64,2048]{1,0:T(8,128)(2,1)} %po_hbm.1, bf16[64,2048]{1,0:T(8,128)(2,1)} %pdo_hbm.1, bf16[64,2048]{1,0:T(8,128)(2,1)} %rq_hbm.1, ...), custom_call_target="tpu_custom_call" | custom-call | tf_op jit(solution)/shard_map/pallas_call | solution.py:467
  60.0 2.1 %shard_map.164 = (f32[64,2048]{1,0:T(8,128)}, f32[64,128]{1,0:T(8,128)}, f32[64,128]{1,0:T(8,128)}, f32[64,2048]{1,0:T(8,128)}, f32[64,128]{1,0:T(8,128)}, /*index=5*/f32[64,128]{1,0:T(8,128)}) custom-call(f32[2,64,2048]{2,1,0:T(8,128)} %get-tuple-element.8.dq_hbm, f32[4,64,128]{2,1,0:T(8,128)} %get-tuple-element.9.kvg_hbm), custom_call_target="tpu_custom_call" | custom-call | tf_op jit(solution)/shard_map/pallas_call | solution.py:510
